TPU v7x, 128 devices: a whole 4x4x4 slice. The times are simulated.
128 devices in a mesh: ctx: 16 (over y, x), head: 8 (over z, core).
Axes of the slice: x: 4, y: 4, z: 4, core: 2. Of those that a mesh axis runs over, the one named last changes fastest.
Arguments:
- queries: bfloat16 [16384, 8192], P('ctx', 'head'), may hold values from -6 to 6
- keys: bfloat16 [16384, 8192], P('ctx', 'head'), may hold values from -6 to 6
- values: bfloat16 [16384, 8192], P('ctx', 'head'), may hold values from -64 to 64
- gate_logits: bfloat16 [16384, 8192], P('ctx', 'head'), may hold values from -6 to 6
- log_decay: float32 [64, 16384], P('head', 'ctx'), may hold values from 0 to 3, as said below
- norm_gain_vector: float32 [8192], P('head'), may hold values from 0.5 to 1.5
- out_weight: bfloat16 [8192, 6144], P('head'), may hold values from -0.0625 to 0.0625
Outputs:
- layer_out: bfloat16 [16384, 6144], P(('ctx', 'head'))
Inputs may be any that keep to these rules, and one draw needn't show every extreme that they name: `log_decay`: log decays are nonnegative.
All inputs are finite; a program needn't handle non-finite values.
Results may differ from a plain program's by a relative error of at most 0.024.
Values may be sent and summed in bfloat16 or wider, within the bound.
A program may use at most 128 MiB of HBM per device.

v0:
```python
import jax
import jax.numpy as jnp
from jax import lax
from jax.sharding import PartitionSpec as P

HEADS = 64
HD = 128
BLOCK = 256


def entering(value, axis, combine, identity):
    count, mine = (lax.axis_size(axis), lax.axis_index(axis))
    everything = jax.tree.map(
        lambda part, kind: lax.all_gather(part.astype(kind), axis),
        value,
        (jnp.bfloat16, jnp.bfloat16),
    )
    start = jax.tree.map(
        lambda part, zero: jnp.broadcast_to(jnp.asarray(zero, part.dtype), part.shape),
        value,
        identity,
    )

    def step(k, before):
        reached = k < mine
        new = combine(
            before, jax.tree.map(lambda part, own: part[k].astype(own.dtype), everything, value)
        )
        return jax.tree.map(lambda a, b: jnp.where(reached, a, b), new, before)

    return lax.fori_loop(0, count, step, start)


def shards(queries, keys, values, gate_logits, log_decay, norm_gain_vector, out_weight):
    hi = lax.Precision.HIGHEST
    tok_rows, width = queries.shape
    heads = log_decay.shape[0]
    blocks = tok_rows // BLOCK
    q_four = queries.reshape(blocks, BLOCK, heads, HD)
    k_four = keys.reshape(blocks, BLOCK, heads, HD)
    v_four = values.reshape(blocks, BLOCK, heads, HD)
    decays = log_decay.reshape(heads, blocks, BLOCK).transpose(1, 0, 2)
    lower = jnp.arange(BLOCK)[:, None] >= jnp.arange(BLOCK)[None, :]
    lowerf = lower.astype(jnp.float32)
    cum = jnp.einsum("bhj,ij->bhi", decays, lowerf, precision=hi)
    diff = cum[:, :, :, None] - cum[:, :, None, :]
    decay = jnp.where(lower[None, None], jnp.exp(-jnp.where(lower[None, None], diff, 0.0)), 0.0)
    scores = jnp.einsum("bihd,bjhd->bhij", q_four, k_four, preferred_element_type=jnp.float32)
    weights = (scores * decay).astype(jnp.bfloat16)
    intra = jnp.einsum("bhij,bjhd->bihd", weights, v_four, preferred_element_type=jnp.float32)
    block_total = cum[:, :, -1]
    key_factor = jnp.exp(-(block_total[:, :, None] - cum)).transpose(0, 2, 1)[..., None]
    kdec = (k_four.astype(jnp.float32) * key_factor).astype(jnp.bfloat16)
    updates = jnp.einsum("bjhd,bjhe->bhde", kdec, v_four, preferred_element_type=jnp.float32)

    def chain(state, inputs):
        update, total = inputs
        return (jnp.exp(-total)[:, None, None] * state + update, state)

    empty = jnp.zeros((heads, HD, HD), jnp.float32)
    local_end, local_start = lax.scan(chain, empty, (updates, block_total))
    shard_total = jnp.sum(block_total, axis=0)
    before = jnp.cumsum(block_total, axis=0) - block_total

    def combine(early, late):
        return (early[0] + late[0], jnp.exp(-late[0])[:, None, None] * early[1] + late[1])

    ident = (jnp.zeros((heads,), jnp.float32), empty)
    prior_decay, carried = entering((shard_total, local_end), "ctx", combine, ident)
    start_states = jnp.exp(-before)[:, :, None, None] * carried[None] + local_start
    query_factor = jnp.exp(-cum).transpose(0, 2, 1)[..., None]
    qdec = (q_four.astype(jnp.float32) * query_factor).astype(jnp.bfloat16)
    inter = jnp.einsum(
        "bihd,bhde->bihe",
        qdec,
        start_states.astype(jnp.bfloat16),
        preferred_element_type=jnp.float32,
    )
    attn = (intra + inter).reshape(tok_rows, width)
    squares = lax.psum(jnp.sum(attn * attn, axis=1), "head")
    scale = lax.rsqrt(squares / (HEADS * HD) + 1e-06)
    hidden = (
        attn
        * scale[:, None]
        * norm_gain_vector[None, :]
        * jax.nn.sigmoid(gate_logits.astype(jnp.float32))
    ).astype(jnp.bfloat16)
    return lax.psum_scatter(
        jnp.dot(hidden, out_weight, preferred_element_type=jnp.float32).astype(jnp.bfloat16),
        "head",
        scatter_dimension=0,
        tiled=True,
    )


def solution(mesh):
    in_specs = (
        P("ctx", "head"),
        P("ctx", "head"),
        P("ctx", "head"),
        P("ctx", "head"),
        P("head", "ctx"),
        P("head"),
        P("head", None),
    )
    out_specs = P(("ctx", "head"), None)
    return jax.shard_map(shards, mesh=mesh, in_specs=in_specs, out_specs=out_specs, check_vma=False)
```

profile of v0, /device:TPU:1, one launch (start us, length us, event | category | flops | bytes accessed | tf_op | source)
XLA Modules:
  0.0 218.9 jit_solution(17882493855824902397)
XLA Ops:
  6.5 0.8 copy-done
  7.3 0.3 fusion.28
  7.6 0.2 slice_reduce_fusion
  7.8 0.1 exponential_bitcast_fusion.2
  7.9 2.2 %copy.29 = bf16[128,8,8,128]{3,2,1,0:T(8,128)(2,1)S(1)} copy(bf16[128,8,8,128]{3,1,2,0:T(8,128)(2,1)} %bitcast.70) | data formatting | bytes 4194304
  10.1 2.6 %copy.22 = bf16[4,256,8,128]{1,3,2,0:T(8,128)(2,1)} copy(bf16[4,256,8,128]{3,2,1,0:T(8,128)(2,1)S(1)} %bitcast.68) | data formatting | bytes 4194304 | tf_op jit(solution)/shard_map/reshape | solution.py:40
  12.7 2.4 %copy.30 = bf16[128,8,8,128]{3,2,1,0:T(8,128)(2,1)S(1)} copy(bf16[128,8,8,128]{3,1,2,0:T(8,128)(2,1)} %bitcast.71) | data formatting | bytes 4194304
  15.1 0.7 fusion.15
  15.8 0.6 copy-done.3
  16.5 4.0 %while.27 = (s32[]{:T(128)}, f32[8,128,128]{2,1,0:T(8,128)S(1)}, f32[4,8,128,128]{3,2,1,0:T(8,128)}, f32[4,8]{1,0:T(4,128)S(1)}, f32[4,8,128,128]{3,2,1,0:T(8,128)S(1)}, /*index=5*/s32[]{:T(128)}, s32[]{:T(128)}) while((s32[]{:T(128)}, f32[8,128,128]{2,1,0:T(8,128)S(1)}, f32[4,8,128,128]{3,2,1,0:T(8,128)}, f32[4,8]{1,0:T(4,128)S(1)}, ...), condition=%wide.region_3.4_spmd.clone, body=%wide.region_2.3_spmd.clone.sunk | while | flops 524299 | bytes 2621644 | solution.py:61
  16.5 0.9 bitcast_dynamic-update-slice_fusion.2
  17.3 0.1 bitcast_add_fusion.3
  17.5 0.9 bitcast_dynamic-update-slice_fusion.2
  18.4 0.1 bitcast_add_fusion.3
  18.5 0.8 bitcast_dynamic-update-slice_fusion.2
  19.4 0.1 bitcast_add_fusion.3
  19.5 0.8 bitcast_dynamic-update-slice_fusion.2
  20.3 0.1 bitcast_add_fusion.3
  20.5 0.7 convert_element_type.71
  21.4 0.6 dynamic-slice
  22.5 0.2 dynamic-update-slice
  22.8 34.4 %all-reduce = bf16[128]{0:T(256)(128)(2,1)S(1)} all-reduce(bf16[128]{0:T(256)(128)(2,1)S(1)} %dynamic-update-slice), channel_id=2, replica_groups=mesh['ctx'=16,'head'=8] {'ctx'}, use_global_device_ids=true, to_apply=%add | all-reduce | flops 128 | bytes 512
  57.2 0.1 reshape.85
  57.3 3.7 %copy.28 = bf16[128,8,8,128]{3,2,1,0:T(8,128)(2,1)} copy(bf16[128,8,8,128]{3,1,2,0:T(8,128)(2,1)} %bitcast.72) | data formatting | bytes 4194304
  61.0 6.5 %fusion.4 = f32[4,8,256,128]{2,3,1,0:T(8,128)} fusion(f32[4,8,256]{2,1,0:T(8,128)S(1)} %bitcast.75, pred[256,256]{1,0:T(8,128)(4,1)S(1)} %iota_compare_fusion, bf16[4,256,8,128]{1,3,2,0:T(8,128)(2,1)S(1)} %copy-done.2, bf16[4,256,8,128]{3,2,1,0:T(8,128)(2,1)} %bitcast.65, bf16[4,256,8,128]{3,2,1,0:T(8,128)(2,1)} %bitcast.66), kind=kOutput, calls=%fused_computation.11 | convolution fusion | flops 1086324736 | bytes 10584064 | tf_op jit(solution)/shard_map/bhij,bjhd->bihd/dot_general | solution.py:50
  67.6 8.5 %all-gather.4.cloned.1.call-done = bf16[128,128,128]{2,1,0:T(8,128)(2,1)} async-done(((bf16[8,128,128]{2,1,0:T(8,128)(2,1)}), bf16[128,128,128]{2,1,0:T(8,128)(2,1)}) %all-gather.4.cloned.1.call-update) | async-done | bytes 4194320 | tf_op jit(solution)/shard_map/all_gather | solution.py:14
  76.1 18.2 %while.28 = (s32[]{:T(128)}, f32[8,128,128]{2,1,0:T(8,128)S(1)}, s32[]{:T(128)}, bf16[16,8]{1,0:T(8,128)(2,1)S(1)}, bf16[16,8,128,128]{3,2,1,0:T(8,128)(2,1)}, /*index=5*/s32[]{:T(128)}, s32[]{:T(128)}) while((s32[]{:T(128)}, f32[8,128,128]{2,1,0:T(8,128)S(1)}, s32[]{:T(128)}, bf16[16,8]{1,0:T(8,128)(2,1)S(1)}, ...), condition=%wide.region_5.6_spmd.clone, body=%wide.region_4.5_spmd.clone.sunk | while | flops 655380 | bytes 1310913 | solution.py:31
  76.1 1.1 fusion.38
  77.2 1.1 fusion.38
  78.4 1.1 fusion.38
  79.5 1.1 fusion.38
  80.7 1.1 fusion.38
  81.8 1.1 fusion.38
  82.9 1.1 fusion.38
  84.1 1.1 fusion.38
  85.2 1.1 fusion.38
  86.3 1.1 fusion.38
  87.5 1.1 fusion.38
  88.6 1.1 fusion.38
  89.8 1.1 fusion.38
  90.9 1.1 fusion.38
  92.0 1.1 fusion.38
  93.2 1.1 fusion.38
  94.3 6.8 %multiply_reduce_fusion = (f32[4,256]{1,0:T(4,128)S(1)}, f32[4,256,8,128]{1,3,2,0:T(8,128)}) fusion(f32[4,256,8]{1,2,0:T(8,128)S(1)} %get-tuple-element.189, bf16[4,256,8,128]{3,2,1,0:T(8,128)(2,1)} %bitcast.67, f32[4,8,128,128]{3,2,1,0:T(8,128)} %get-tuple-element.129, f32[8,128,128]{2,1,0:T(8,128)S(1)} %get-tuple-element.128, ...), kind=kOutput, calls=%fused_computation.17 | convolution fusion | flops 276298752 | bytes 13144192 | tf_op jit(solution)/shard_map/bihd,bhde->bihe/dot_general | solution.py:73
  101.1 12.8 %psum.7 = f32[1024]{0:T(1024)S(1)} all-reduce(f32[1024]{0:T(1024)S(1)} %bitcast.77), channel_id=1, replica_groups=mesh['ctx'=16,'head'=8] {'head'}, use_global_device_ids=true, to_apply=%region_7.8 | all-reduce | flops 1024 | bytes 8192 | tf_op jit(solution)/shard_map/psum | solution.py:80
  113.9 5.4 %copy.26 = f32[4,256,8,128]{3,2,1,0:T(8,128)} copy(f32[4,256,8,128]{1,3,2,0:T(8,128)} %get-tuple-element.191) | data formatting | bytes 8388608 | tf_op jit(solution)/shard_map/add | solution.py:79
  119.3 21.4 %convolution_convert_fusion = bf16[1024,6144]{1,0:T(8,128)(2,1)} fusion(bf16[1024,6144]{1,0:T(8,128)(2,1)} %param.17, f32[128,8,8,128]{3,2,1,0:T(8,128)} %bitcast.69, bf16[1024,1024]{1,0:T(8,128)(2,1)S(1)} %copy-done.4, f32[1024]{0:T(1024)S(1)} %copy-done.5, f32[1024]{0:T(1024)S(1)} %add_rsqrt_fusion), kind=kOutput, calls=%fused_computation.9 | convolution fusion | flops 12899581952 | bytes 31465472 | tf_op jit(solution)/shard_map/dot_general | solution.py:89
  140.8 71.3 %reduce-scatter.2.cloned.1.call-done = bf16[128,6144]{1,0:T(8,128)(2,1)} async-done(((bf16[1024,6144]{1,0:T(8,128)(2,1)}), bf16[128,6144]{1,0:T(8,128)(2,1)}) %reduce-scatter.2.cloned.1.call-update) | async-done | bytes 1572880 | tf_op jit(solution)/shard_map/reduce_scatter | solution.py:88
  (45 shorter events, 0.4 us)
Async XLA Ops:
  6.5 0.8 copy-start
  6.5 69.6 %all-gather.4.cloned.1.call-start = ((), (), s32[]{:S(2)}) async-start(), calls=%async_computation.2 | async-start | bytes 4456448 | tf_op jit(solution)/shard_map/all_gather | solution.py:14
  12.7 2.4 %copy-start.1 = (bf16[4,256,8,128]{1,3,2,0:T(8,128)(2,1)S(1)}, bf16[4,256,8,128]{1,3,2,0:T(8,128)(2,1)}, u32[]{:S(2)}) copy-start(bf16[4,256,8,128]{1,3,2,0:T(8,128)(2,1)} %copy.22) | copy-start | bytes 6291460
  15.1 1.4 copy-start.3
  16.4 4.9 %copy-start.6 = (u32[128]{0:T(128)S(1)}, u32[128]{0:T(128)}, u32[]{:S(2)}) copy-start(u32[128]{0:T(128)} %constant.57) | copy-start | bytes 1540
  21.2 190.8 %reduce-scatter.2.cloned.1.call-start = ((), (), s32[]{:S(2)}) async-start(), calls=%async_computation.1 | async-start | bytes 14155776 | tf_op jit(solution)/shard_map/reduce_scatter | solution.py:88
  57.3 3.7 %copy-start.2 = (bf16[4,256,8,128]{1,3,2,0:T(8,128)(2,1)S(1)}, bf16[4,256,8,128]{1,3,2,0:T(8,128)(2,1)}, u32[]{:S(2)}) copy-start(bf16[4,256,8,128]{1,3,2,0:T(8,128)(2,1)} %copy.22) | copy-start | bytes 6291460
  113.9 5.5 %copy-start.4 = (bf16[1024,1024]{1,0:T(8,128)(2,1)S(1)}, bf16[1024,1024]{1,0:T(8,128)(2,1)}, u32[]{:S(2)}) copy-start(bf16[1024,1024]{1,0:T(8,128)(2,1)} %param.14) | copy-start | bytes 6291460
  113.9 5.4 %copy-start.5 = (f32[1024]{0:T(1024)S(1)}, f32[1024]{0:T(1024)}, u32[]{:S(2)}) copy-start(f32[1024]{0:T(1024)} %param.16) | copy-start | bytes 12292
Sparse Core Ops, SparseCore 0:
  21.4 54.6 all-gather.3
  140.9 71.1 reduce-scatter.1
where the time goes:
time: 220 us; the launch traced here: 219 us
  waiting for transfers between devices  79.9 us (36%)
  blocking collectives  47.2 us (21%)
  matrix products  35.8 us (16%)
  other arithmetic  22.8 us (10%)
  local copies, waits for them, and re-layouts  18.6 us (8%)
  between operations  14.2 us (6%)
    reduce_scatter x1, waiting for transfers between devices, shards(): lax.psum_scatter(jnp.dot(hidden, out_weight, preferred_element_type=jnp.f...  71.3 us
    unnamed x1, blocking collectives  34.4 us
    dot_general x1, matrix products, shards(): jnp.dot(hidden, out_weight, preferred_element_type=jnp.float32)  21.4 us
    select_n x16, other arithmetic, step(): return jax.tree.map(lambda a, b: jnp.where(reached, a, b), new, before)  17.5 us
    psum x1, blocking collectives, shards(): squares = lax.psum(jnp.sum(attn * attn, axis=1), 'head')  12.8 us
    unnamed x21, local copies, waits for them, and re-layouts  10.5 us
    all_gather x1, waiting for transfers between devices, entering(): lax.all_gather(part.astype(kind), axis)  8.52 us
    dot_general x1, matrix products, shards(): jnp.einsum('bihd,bhde->bihe', qdec, start_states.astype(jnp.bfloat16), pr...  6.81 us
  transfers between devices with their start and end apart: 2, of which 2 were waited for; matrix products, arithmetic and copies ran while one was open for 5% of the time, Pallas kernels for 0%

commit v1 on v0

v1 whole, which is shorter than its diff:
```python
import functools

import jax
import jax.numpy as jnp
from jax import lax
from jax.experimental import pallas as pl
from jax.experimental.pallas import tpu as pltpu
from jax.sharding import PartitionSpec as P

HEADS = 64
HD = 128
BLOCK = 256
EPS = 1e-06

N_CTX = 16
N_HEAD = 8
ROWS = 1024
WIDTH = 1024
D = 6144
LH = 8
NB = 4
HALF = 128
CN = 512
NC = D // CN
NH = NC // 2
SL = LH * HD // N_CTX
MSG = SL + 16

F32 = jnp.float32
BF16 = jnp.bfloat16
HI = lax.Precision.HIGHEST


def ds(start, size):
    return pl.ds(pl.multiple_of(start * size, size), size)


def kernel(
    q_hbm, k_hbm, v_hbm, gate_hbm, decay_ref, gain_ref, w_hbm, out_hbm,
    q_v, k_v, v_v, gate_v, w_v, hid, intra, gated, local, cur,
    cum_row, cum_col, dec_col, before_dec,
    scan_out, scan_in, prefix_out, prefix_in, ssq_out, ssq_in,
    core_out, core_in, own, z_out, far_in, near_in, total, out_v,
    load_sem, w_sem, out_sem, scan_ssem, scan_rsem, pre_ssem, pre_rsem,
    ssq_ssem, ssq_rsem, core_ssem, core_rsem, z_ssem, far_rsem, near_rsem,
):
    ctx = lax.axis_index("ctx")
    head = lax.axis_index("head")
    z = head // 2
    core = head % 2
    partner = z * 2 + (1 - core)
    zr = (z + 1) % 4
    zl = (z + 3) % 4
    zo = (z + 2) % 4
    right = zr * 2 + core
    left = zl * 2 + core

    def load(src, dst, sem):
        return pltpu.make_async_copy(src, dst, sem)

    def block_load(i, src, dst, b):
        return load(src.at[ds(b, BLOCK)], dst.at[ds(b, BLOCK)], load_sem.at[i, b])

    def w_load(n):
        return load(w_hbm.at[:, ds(n, CN)], w_v.at[n], w_sem.at[n])

    for b in range(NB):
        block_load(0, k_hbm, k_v, b).start()
        block_load(1, v_hbm, v_v, b).start()

    barrier = pltpu.get_barrier_semaphore()

    def greet_ctx(d, _):
        pl.semaphore_signal(barrier, inc=1, device_id={"ctx": (ctx + d) % N_CTX},
                            device_id_type=pl.DeviceIdType.MESH)
        return 0

    def greet_head(d, _):
        pl.semaphore_signal(barrier, inc=1, device_id={"head": (head + d) % N_HEAD},
                            device_id_type=pl.DeviceIdType.MESH)
        return 0

    lax.fori_loop(1, N_CTX, greet_ctx, 0)
    lax.fori_loop(1, N_HEAD, greet_head, 0)

    for b in range(NB):
        block_load(2, q_hbm, q_v, b).start()

    ri = lax.broadcasted_iota(jnp.int32, (BLOCK, BLOCK), 0)
    ci = lax.broadcasted_iota(jnp.int32, (BLOCK, BLOCK), 1)
    lower = (ri >= ci).astype(F32)
    nt = (((1,), (1,)), ((), ()))
    tn = (((0,), (0,)), ((), ()))
    before = jnp.zeros((1, LH), F32)
    for b in range(NB):
        dec = decay_ref[:, b * BLOCK:(b + 1) * BLOCK]
        row = lax.dot_general(dec, lower, nt, precision=HI, preferred_element_type=F32)
        col = lax.dot_general(lower, dec, nt, precision=HI, preferred_element_type=F32)
        cum_row[b] = row
        cum_col[b] = col
        dec_col[b] = jnp.exp(-col)
        before_dec[b, 0:1, :] = jnp.exp(-before)
        before = before + col[BLOCK - 1:BLOCK, :]
    shard_dec = jnp.exp(-before)

    cur[...] = jnp.zeros_like(cur)

    def update(b, _):
        block_load(0, k_hbm, k_v, b).wait()
        block_load(1, v_hbm, v_v, b).wait()
        col = cum_col[b]
        last = col[BLOCK - 1:BLOCK, :]
        factor = jnp.exp(col - last)
        carry = jnp.exp(-last)
        for h in range(LH):
            kb = k_v[ds(b, BLOCK), h * HD:(h + 1) * HD].astype(F32)
            vb = v_v[ds(b, BLOCK), h * HD:(h + 1) * HD]
            kd = (kb * factor[:, h:h + 1]).astype(BF16)
            new = lax.dot_general(kd, vb, tn, preferred_element_type=F32)
            old = cur[h]
            local[b, h] = old
            cur[h] = carry[:, h:h + 1] * old + new
        return 0

    lax.fori_loop(0, NB, update, 0)

    tile = lax.broadcasted_iota(jnp.int32, (16, HD), 0)
    for h in range(LH):
        a = jnp.broadcast_to(shard_dec[:, h:h + 1], (16, HD))
        hi = a.astype(BF16).astype(F32)
        mid = (a - hi).astype(BF16).astype(F32)
        low = a - hi - mid
        parts = jnp.where(tile == 0, hi, jnp.where(tile == 1, mid, jnp.where(tile == 2, low, 0.0)))
        parts = parts.astype(BF16)
        for s in range(2):
            scan_out[2 * h + s, 0:SL] = cur[h, s * SL:(s + 1) * SL].astype(BF16)
            scan_out[2 * h + s, SL:MSG] = parts

    pl.semaphore_wait(barrier, N_CTX - 1 + N_HEAD - 1)

    def scan_copy(there, slot):
        return pltpu.make_async_remote_copy(
            src_ref=scan_out.at[there], dst_ref=scan_in.at[slot],
            send_sem=scan_ssem.at[there], recv_sem=scan_rsem.at[slot],
            device_id={"ctx": there}, device_id_type=pl.DeviceIdType.MESH)

    def prefix_copy(there, slot):
        return pltpu.make_async_remote_copy(
            src_ref=prefix_out.at[there], dst_ref=prefix_in.at[slot],
            send_sem=pre_ssem.at[there], recv_sem=pre_rsem.at[slot],
            device_id={"ctx": there}, device_id_type=pl.DeviceIdType.MESH)

    def scan_send(d, _):
        scan_copy((ctx + d) % N_CTX, ctx).start()
        return 0

    lax.fori_loop(1, N_CTX, scan_send, 0)
    scan_in[ctx] = scan_out[ctx]

    for j in range(NH):
        w_load(j).start()
        w_load(NH + j).start()
    for b in range(NB):
        block_load(3, gate_hbm, gate_v, b).start()

    r2 = lax.broadcasted_iota(jnp.int32, (HALF, HALF), 0)
    c2 = lax.broadcasted_iota(jnp.int32, (HALF, HALF), 1)
    keep = r2 >= c2

    def inside(b, _):
        block_load(2, q_hbm, q_v, b).wait()
        rows = cum_row[b]
        cols = cum_col[b]
        for h in range(LH):
            lanes = slice(h * HD, (h + 1) * HD)
            qb = q_v[ds(b, BLOCK), lanes]
            kb = k_v[ds(b, BLOCK), lanes]
            vb = v_v[ds(b, BLOCK), lanes]
            scores = lax.dot_general(qb, kb, nt, preferred_element_type=F32)
            cr = rows[h:h + 1, :]
            cc = jnp.broadcast_to(cols[:, h:h + 1], (BLOCK, HALF))
            top = jnp.where(keep, scores[:HALF, :HALF] * jnp.exp(cr[:, :HALF] - cc[:HALF]), 0.0)
            bl = scores[HALF:, :HALF] * jnp.exp(cr[:, :HALF] - cc[HALF:])
            br = jnp.where(keep, scores[HALF:, HALF:] * jnp.exp(cr[:, HALF:] - cc[HALF:]), 0.0)
            a0 = jnp.dot(top.astype(BF16), vb[:HALF], preferred_element_type=F32)
            bottom = jnp.concatenate([bl.astype(BF16), br.astype(BF16)], axis=1)
            a1 = jnp.dot(bottom, vb, preferred_element_type=F32)
            intra[b, :HALF, lanes] = a0
            intra[b, HALF:, lanes] = a1
        return 0

    lax.fori_loop(0, 2, inside, 0)

    def prefix(s, state):
        @pl.when(s != ctx)
        def _():
            scan_copy(ctx, s).wait_recv()

        prefix_out[s] = state.astype(BF16)

        @pl.when(s != ctx)
        def _():
            prefix_copy(s, ctx).start()

        dec = jnp.sum(scan_in[s, SL:MSG].astype(F32), axis=0, keepdims=True)
        return dec * state + scan_in[s, 0:SL].astype(F32)

    lax.fori_loop(0, N_CTX, prefix, jnp.zeros((SL, HD), F32))
    prefix_in[ctx] = prefix_out[ctx]

    lax.fori_loop(2, NB, inside, 0)

    def gating(b, _):
        block_load(3, gate_hbm, gate_v, b).wait()
        for h in range(LH):
            lanes = slice(h * HD, (h + 1) * HD)
            gl = gate_v[ds(b, BLOCK), lanes].astype(F32)
            gated[b, :, lanes] = jax.nn.sigmoid(gl) * gain_ref[:, lanes]
        return 0

    lax.fori_loop(0, NB, gating, 0)

    def prefix_wait(d, _):
        prefix_copy(ctx, (ctx + d) % N_CTX).wait_recv()
        return 0

    lax.fori_loop(1, N_CTX, prefix_wait, 0)

    ones = jnp.ones((8, HD), F32)

    def ssq_copy(there, slot):
        return pltpu.make_async_remote_copy(
            src_ref=ssq_out.at[there], dst_ref=ssq_in.at[slot],
            send_sem=ssq_ssem.at[there], recv_sem=ssq_rsem.at[slot],
            device_id={"head": there}, device_id_type=pl.DeviceIdType.MESH)

    def finish(rb):
        dc = dec_col[rb]
        bd = before_dec[rb]
        square = jnp.zeros((BLOCK, HD), F32)
        for h in range(LH):
            lanes = slice(h * HD, (h + 1) * HD)
            carried = jnp.concatenate([prefix_in[2 * h], prefix_in[2 * h + 1]], axis=0)
            start = (bd[0:1, h:h + 1] * carried.astype(F32) + local[rb, h]).astype(BF16)
            inter = jnp.dot(q_v[ds(rb, BLOCK), lanes], start, preferred_element_type=F32)
            attn = intra[rb, :, lanes] + dc[:, h:h + 1] * inter
            square = square + attn * attn
            hidden = (attn * gated[rb, :, lanes]).astype(BF16)
            hid[rb, ds(1 - core, HALF), lanes] = hidden[:HALF]
            hid[rb, ds(core, HALF), lanes] = hidden[HALF:]
        sums = lax.dot_general(ones, square, nt, precision=HI, preferred_element_type=F32)
        for s in range(2):
            there = rb * 2 + s
            ssq_out[there] = sums[:, s * HALF:(s + 1) * HALF]

            @pl.when(there != head)
            def _():
                ssq_copy(there, head).start()

            @pl.when(there == head)
            def _():
                ssq_in[head] = ssq_out[head]

    def core_copy(slot):
        return pltpu.make_async_remote_copy(
            src_ref=core_out.at[slot], dst_ref=core_in.at[slot],
            send_sem=core_ssem.at[slot], recv_sem=core_rsem.at[slot],
            device_id={"head": partner}, device_id_type=pl.DeviceIdType.MESH)

    def far_copy(n, there):
        return pltpu.make_async_remote_copy(
            src_ref=z_out.at[0, n], dst_ref=far_in.at[n],
            send_sem=z_ssem.at[0, n], recv_sem=far_rsem.at[n],
            device_id={"head": there}, device_id_type=pl.DeviceIdType.MESH)

    def near_copy(side, n, there):
        return pltpu.make_async_remote_copy(
            src_ref=z_out.at[1 + side, n], dst_ref=near_in.at[side, n],
            send_sem=z_ssem.at[1 + side, n], recv_sem=near_rsem.at[side, n],
            device_id={"head": there}, device_id_type=pl.DeviceIdType.MESH)

    def product(phase, lane, rb, n):
        slot = phase * NC + n
        r = jnp.dot(hid[rb], w_v[n], preferred_element_type=F32)
        core_out[slot] = r[:HALF].astype(BF16)
        core_copy(slot).start()
        return r[HALF:]

    def summed(phase, lane, n):
        slot = phase * NC + n
        core_copy(slot).wait_recv()
        return own[lane] + core_in[slot].astype(F32)

    def fin0(lane, j):
        n = lane * NH + j
        z_out[0, n] = summed(0, lane, n).astype(BF16)
        far_copy(n, right if lane == 0 else left).start()

    def fin1(lane, j):
        n = (1 - lane) * NH + j
        z_out[1 + lane, n] = summed(1, lane, n).astype(BF16)
        near_copy(lane, n, right if lane == 0 else left).start()

    def fin2(lane, j):
        n = lane * NH + j
        s = summed(2, lane, n)
        far_copy(n, right if lane == 0 else left).wait_recv()
        z_out[1 + lane, n] = (s + far_in[n].astype(F32)).astype(BF16)
        near_copy(lane, n, right if lane == 0 else left).start()

    def fin3(lane, j):
        n = lane * NH + j
        total[n] = summed(3, lane, n)

    def step(phase, lane, j):
        n = (1 - lane) * NH + j if phase == 1 else lane * NH + j
        if phase == 0:
            rb = zo
        elif phase == 3:
            rb = z
        else:
            rb = zr if lane == 0 else zl
        if phase == 0:
            w_load(n).wait()
        return product(phase, lane, rb, n)

    fins = (fin0, fin1, fin2, fin3)
    pending = None
    for phase in range(4):
        if phase == 0:
            finish(zo)
        elif phase == 1:
            finish(zr)
            finish(zl)
        elif phase == 3:
            finish(z)
        for lane in range(2):
            r = step(phase, lane, 0)
            if pending is not None:
                pending(lane, NH - 1)
            own[lane] = r

        def body(j, _, phase=phase):
            for lane in range(2):
                r = step(phase, lane, j)
                fins[phase](lane, j - 1)
                own[lane] = r
            return 0

        lax.fori_loop(1, NH, body, 0)
        pending = fins[phase]
    for lane in range(2):
        pending(lane, NH - 1)

    def ssq_wait(d, _):
        ssq_copy(head, (head + d) % N_HEAD).wait_recv()
        return 0

    lax.fori_loop(1, N_HEAD, ssq_wait, 0)
    squares = jnp.sum(ssq_in[...], axis=0)
    scale_row = lax.rsqrt(squares[0:1, :] * (1.0 / (HEADS * HD)) + EPS)
    scale = jnp.sum(
        jnp.where(r2 == c2, jnp.broadcast_to(scale_row, (HALF, HALF)), 0.0), axis=1, keepdims=True)

    def out_copy(n):
        return load(out_v.at[n], out_hbm.at[:, ds(n, CN)], out_sem.at[n])

    def result(j, _):
        for lane in range(2):
            n = lane * NH + j
            near_copy(0, n, right).wait_recv()
            near_copy(1, n, left).wait_recv()
            s = total[n] + near_in[0, n].astype(F32) + near_in[1, n].astype(F32)
            out_v[n] = (s * scale).astype(BF16)
            out_copy(n).start()
        return 0

    lax.fori_loop(0, NH, result, 0)

    def drain_scan(d, _):
        scan_copy((ctx + d) % N_CTX, ctx).wait_send()
        prefix_copy((ctx + d) % N_CTX, ctx).wait_send()
        return 0

    def drain_ssq(d, _):
        ssq_copy((head + d) % N_HEAD, head).wait_send()
        return 0

    def drain_core(s, _):
        core_copy(s).wait_send()
        return 0

    def drain_z(n, _):
        far_copy(n, right).wait_send()
        near_copy(0, n, right).wait_send()
        near_copy(1, n, left).wait_send()
        return 0

    lax.fori_loop(1, N_CTX, drain_scan, 0)
    lax.fori_loop(1, N_HEAD, drain_ssq, 0)
    lax.fori_loop(0, 4 * NC, drain_core, 0)
    lax.fori_loop(0, NC, drain_z, 0)

    def drain_out(n, _):
        out_copy(n).wait()
        return 0

    lax.fori_loop(0, NC, drain_out, 0)


def shards(queries, keys, values, gate_logits, log_decay, norm_gain_vector, out_weight):
    any_spec = pl.BlockSpec(memory_space=pl.ANY)
    vmem = pl.BlockSpec(memory_space=pltpu.VMEM)
    dma = pltpu.SemaphoreType.DMA
    return pl.pallas_call(
        kernel,
        out_shape=jax.ShapeDtypeStruct((ROWS // N_HEAD, D), BF16),
        in_specs=[any_spec] * 4 + [vmem, vmem, any_spec],
        out_specs=any_spec,
        scratch_shapes=[
            pltpu.VMEM((ROWS, WIDTH), BF16),
            pltpu.VMEM((ROWS, WIDTH), BF16),
            pltpu.VMEM((ROWS, WIDTH), BF16),
            pltpu.VMEM((ROWS, WIDTH), BF16),
            pltpu.VMEM((NC, WIDTH, CN), BF16),
            pltpu.VMEM((NB, BLOCK, WIDTH), BF16),
            pltpu.VMEM((NB, BLOCK, WIDTH), F32),
            pltpu.VMEM((NB, BLOCK, WIDTH), F32),
            pltpu.VMEM((NB, LH, HD, HD), F32),
            pltpu.VMEM((LH, HD, HD), F32),
            pltpu.VMEM((NB, LH, BLOCK), F32),
            pltpu.VMEM((NB, BLOCK, LH), F32),
            pltpu.VMEM((NB, BLOCK, LH), F32),
            pltpu.VMEM((NB, 8, LH), F32),
            pltpu.VMEM((N_CTX, MSG, HD), BF16),
            pltpu.VMEM((N_CTX, MSG, HD), BF16),
            pltpu.VMEM((N_CTX, SL, HD), BF16),
            pltpu.VMEM((N_CTX, SL, HD), BF16),
            pltpu.VMEM((N_HEAD, 8, HALF), F32),
            pltpu.VMEM((N_HEAD, 8, HALF), F32),
            pltpu.VMEM((4 * NC, HALF, CN), BF16),
            pltpu.VMEM((4 * NC, HALF, CN), BF16),
            pltpu.VMEM((2, HALF, CN), F32),
            pltpu.VMEM((3, NC, HALF, CN), BF16),
            pltpu.VMEM((NC, HALF, CN), BF16),
            pltpu.VMEM((2, NC, HALF, CN), BF16),
            pltpu.VMEM((NC, HALF, CN), F32),
            pltpu.VMEM((NC, HALF, CN), BF16),
            dma((4, NB)), dma((NC,)), dma((NC,)),
            dma((N_CTX,)), dma((N_CTX,)), dma((N_CTX,)), dma((N_CTX,)),
            dma((N_HEAD,)), dma((N_HEAD,)),
            dma((4 * NC,)), dma((4 * NC,)),
            dma((3, NC)), dma((NC,)), dma((2, NC)),
        ],
        compiler_params=pltpu.CompilerParams(
            collective_id=0, has_side_effects=True, vmem_limit_bytes=63 * 1024 * 1024),
        cost_estimate=pl.CostEstimate(
            flops=15_000_000_000, bytes_accessed=23_000_000, transcendentals=4_000_000),
        name="attention",
    )(queries, keys, values, gate_logits, log_decay, norm_gain_vector.reshape(1, WIDTH), out_weight)


def solution(mesh):
    in_specs = (
        P("ctx", "head"),
        P("ctx", "head"),
        P("ctx", "head"),
        P("ctx", "head"),
        P("head", "ctx"),
        P("head"),
        P("head", None),
    )
    out_specs = P(("ctx", "head"), None)
    return jax.shard_map(shards, mesh=mesh, in_specs=in_specs, out_specs=out_specs, check_vma=False)
```

time: 220 us -> 85.3 us (0.39)
  Pallas kernels: 0 us -> 82.4 us
  waiting for transfers between devices: 79.9 us -> 0 us
  blocking collectives: 47.2 us -> 0 us
  matrix products: 35.8 us -> 0 us
  other arithmetic: 22.8 us -> 0 us
  local copies, waits for them, and re-layouts: 18.6 us -> 2.69 us
  between operations: 14.2 us -> 0.01 us
    pallas_call x0 -> x1, Pallas kernels: none -> 82.4 us  [shards(): pl.pallas_call(kernel, out_shape=jax.ShapeDtypeStruct((ROWS // N_HEAD, D)...]
    reduce_scatter x1 -> x0, waiting for transfers between devices: 71.3 us -> none  [shards(): lax.psum_scatter(jnp.dot(hidden, out_weight, preferred_element_type=jnp.f...]
    dot_general x5 -> x0, matrix products: 35.8 us -> none  [the longest x1 21.4 us: shards(): jnp.dot(hidden, out_weight, preferred_element_type=jnp.float32)]
    unnamed x1 -> x0, blocking collectives: 34.4 us -> none
    select_n x16 -> x0, other arithmetic: 17.5 us -> none  [step(): return jax.tree.map(lambda a, b: jnp.where(reached, a, b), new, before)]
    psum x1 -> x0, blocking collectives: 12.8 us -> none  [shards(): squares = lax.psum(jnp.sum(attn * attn, axis=1), 'head')]
    all_gather x1 -> x0, waiting for transfers between devices: 8.52 us -> none  [entering(): lax.all_gather(part.astype(kind), axis)]
    unnamed x21 -> x1, local copies, waits for them, and re-layouts: 10.5 us -> 2.69 us
  transfers between devices with their start and end apart: 2 -> 0, of which waited for: 2 -> 0; matrix products, arithmetic and copies ran while one was open for 5% -> 0% of each run, Pallas kernels for 0% -> 0%
where the time goes in v1:
time: 85.3 us; the launch traced here: 85.1 us
  Pallas kernels  82.4 us (97%)
  local copies, waits for them, and re-layouts  2.69 us (3%)
    pallas_call x1, Pallas kernels, shards(): pl.pallas_call(kernel, out_shape=jax.ShapeDtypeStruct((ROWS // N_HEAD, D)...  82.4 us
    unnamed x1, local copies, waits for them, and re-layouts  2.69 us

profile of v1, /device:TPU:1, one launch (start us, length us, event | category | flops | bytes accessed | tf_op | source)
XLA Modules:
  0.0 85.1 jit_solution(15250228726821405719)
XLA Ops:
  0.0 82.4 %attention.1 = bf16[128,6144]{1,0:T(8,128)(2,1)} custom-call(bf16[1024,1024]{1,0:T(8,128)(2,1)} %q_hbm.1, bf16[1024,1024]{1,0:T(8,128)(2,1)} %k_hbm.1, bf16[1024,1024]{1,0:T(8,128)(2,1)} %v_hbm.1, bf16[1024,1024]{1,0:T(8,128)(2,1)} %gate_hbm.1, f32[8,1024]{1,0:T(8,128)} %decay_ref.1, f32[1,1024]{1,0:T(1,128)} %bitcast.1, bf16[1024,6144]{1,0:T(8,128)(2,1)} %w_hbm.1), custom_call_target="tpu_custom_call" | custom-call | flops 15000000512 | bytes 23000000 | tf_op jit(solution)/shard_map/attention/pallas_call | solution.py:415
  82.4 2.7 %copy.9 = bf16[128,6144]{1,0:T(8,128)(2,1)} copy(bf16[128,6144]{1,0:T(8,128)(2,1)} %attention.1) | data formatting | bytes 3145728

commit v2 on v1

v2 whole, which is shorter than its diff:
```python
import functools

import jax
import jax.numpy as jnp
from jax import lax
from jax.experimental import pallas as pl
from jax.experimental.pallas import tpu as pltpu
from jax.sharding import PartitionSpec as P

HEADS = 64
HD = 128
BLOCK = 256
EPS = 1e-06

N_CTX = 16
N_HEAD = 8
ROWS = 1024
WIDTH = 1024
D = 6144
LH = 8
NB = 4
HALF = 128
PAIR = 2 * HD
CN = 512
NC = D // CN
NH = NC // 2
SL = LH * HD // N_CTX
MSG = SL + 16

F32 = jnp.float32
BF16 = jnp.bfloat16
HI = lax.Precision.HIGHEST


def ds(start, size):
    return pl.ds(pl.multiple_of(start * size, size), size)


def kernel(
    q_hbm, k_hbm, v_hbm, gate_hbm, decay_hbm, gain_hbm, w_hbm, out_ref,
    decay_ref, gain_ref,
    q_v, k_v, v_v, gate_v, w_v, hid, intra, gated, local,
    cum_row, cum_col, dec_col, before_dec, factor, keep_dec, parts,
    scan_out, scan_in, prefix_out, prefix_in, ssq_out, ssq_in,
    core_out, core_in, own, z_out, far_in, near_in,
    load_sem, once_sem, scan_sem, core_ssem, core_rsem, z_ssem, far_rsem, early_rsem, late_rsem,
):
    ctx = lax.axis_index("ctx")
    head = lax.axis_index("head")
    z = head // 2
    core = head % 2
    partner = z * 2 + (1 - core)
    zr = (z + 1) % 4
    zl = (z + 3) % 4
    zo = (z + 2) % 4
    right = zr * 2 + core
    left = zl * 2 + core

    def load(src, dst, sem):
        return pltpu.make_async_copy(src, dst, sem)

    def block_load(i, src, dst, b):
        return load(src.at[ds(b, BLOCK)], dst.at[ds(b, BLOCK)], load_sem.at[i, b])

    def w_load(n):
        return load(w_hbm.at[:, ds(n, CN)], w_v.at[n], once_sem.at[4])

    q_load = load(q_hbm, q_v, once_sem.at[0])
    gate_load = load(gate_hbm, gate_v, once_sem.at[1])
    decay_load = load(decay_hbm, decay_ref, once_sem.at[2])
    gain_load = load(gain_hbm, gain_ref, once_sem.at[3])
    decay_load.start()

    def all_of(ref, sem):
        load(ref, ref, sem).wait()

    ctx_y = ctx // 4
    ctx_x = ctx % 4
    far_first = (2, 1, 3, 0)
    pairs = [(ctx_y + off) % 4 for off in far_first]
    for b in range(NB):
        block_load(0, k_hbm, k_v, b).start()
        block_load(1, v_hbm, v_v, b).start()

    barrier = pltpu.get_barrier_semaphore()

    def greet_ctx(d, _):
        pl.semaphore_signal(barrier, inc=1, device_id={"ctx": (ctx + d) % N_CTX},
                            device_id_type=pl.DeviceIdType.MESH)
        return 0

    def greet_head(d, _):
        pl.semaphore_signal(barrier, inc=1, device_id={"head": (head + d) % N_HEAD},
                            device_id_type=pl.DeviceIdType.MESH)
        return 0

    lax.fori_loop(1, N_CTX, greet_ctx, 0)
    lax.fori_loop(1, N_HEAD, greet_head, 0)

    ri = lax.broadcasted_iota(jnp.int32, (BLOCK, BLOCK), 0)
    ci = lax.broadcasted_iota(jnp.int32, (BLOCK, BLOCK), 1)
    lower = (ri >= ci).astype(F32)
    eye = (ri == ci).astype(BF16)
    nt = (((1,), (1,)), ((), ()))
    before = jnp.zeros((LH, 1), F32)
    decay_load.wait()
    tile = lax.broadcasted_iota(jnp.int32, (16, HD), 0)
    for b in range(NB):
        dec = decay_ref[:, b * BLOCK:(b + 1) * BLOCK]
        row = lax.dot_general(dec, lower, nt, precision=HI, preferred_element_type=F32)
        cum_row[b] = row
        last = row[:, BLOCK - 1:BLOCK]
        fac = jnp.exp(row - last)
        kept = jnp.broadcast_to(jnp.exp(-last), (LH, HD))
        before_dec[b] = jnp.broadcast_to(jnp.exp(-before), (LH, HD))
        before = before + last
        for p in range(4):
            factor[b, p] = fac[2 * p:2 * p + 2]
            keep_dec[b, p] = kept[2 * p:2 * p + 2]
    shard_dec = jnp.broadcast_to(jnp.exp(-before), (LH, HD))
    for h in range(LH):
        a = jnp.broadcast_to(shard_dec[h:h + 1], (16, HD))
        hi = a.astype(BF16).astype(F32)
        mid = (a - hi).astype(BF16).astype(F32)
        low = a - hi - mid
        part = jnp.where(tile == 0, hi, jnp.where(tile == 1, mid, jnp.where(tile == 2, low, 0.0)))
        parts[h // 2, h % 2] = part.astype(BF16)

    def scan_copy(there, slot):
        return pltpu.make_async_remote_copy(
            src_ref=scan_out.at[there], dst_ref=scan_in.at[slot],
            send_sem=scan_sem.at[0], recv_sem=scan_sem.at[1],
            device_id={"ctx": there}, device_id_type=pl.DeviceIdType.MESH)

    def prefix_copy(there, slot):
        return pltpu.make_async_remote_copy(
            src_ref=prefix_out.at[there], dst_ref=prefix_in.at[slot],
            send_sem=scan_sem.at[2], recv_sem=scan_sem.at[3],
            device_id={"ctx": there}, device_id_type=pl.DeviceIdType.MESH)

    def added(b, p):
        rows = slice(b * BLOCK, (b + 1) * BLOCK)
        lanes = ds(p, PAIR)
        flipped = lax.dot_general(eye, k_v[rows, lanes], nt, preferred_element_type=F32)
        vb = v_v[rows, lanes]
        new = []
        for s in range(2):
            kd = (flipped[s * HD:(s + 1) * HD] * factor[b, p, s:s + 1, :]).astype(BF16)
            new.append(jnp.dot(kd, vb[:, s * HD:(s + 1) * HD], preferred_element_type=F32))
        return new

    for b in range(NB - 1):
        block_load(0, k_hbm, k_v, b).wait()
        block_load(1, v_hbm, v_v, b).wait()
        for p in range(4):
            for s, new in enumerate(added(b, p)):
                if b == 0:
                    local[0, p, s] = jnp.zeros((HD, HD), F32)
                else:
                    new = new + keep_dec[b, p, s:s + 1, :] * local[b, p, s]
                local[b + 1, p, s] = new

    block_load(0, k_hbm, k_v, NB - 1).wait()
    block_load(1, v_hbm, v_v, NB - 1).wait()
    q_load.start()

    for i, p in enumerate(pairs):
        for s, new in enumerate(added(NB - 1, p)):
            state = new + keep_dec[NB - 1, p, s:s + 1, :] * local[NB - 1, p, s]
            for t in range(2):
                scan_out[4 * p + 2 * s + t, 0:SL] = state[t * SL:(t + 1) * SL].astype(BF16)
                scan_out[4 * p + 2 * s + t, SL:MSG] = parts[p, s]
        if i == 0:
            pl.semaphore_wait(barrier, N_CTX - 1 + N_HEAD - 1)
        for off in far_first:
            there = 4 * p + (ctx_x + off) % 4
            if far_first[i] == 0 and off == 0:
                scan_in[ctx] = scan_out[ctx]
            else:
                scan_copy(there, ctx).start()

    for j in range(NH):
        w_load(j).start()
        w_load(NH + j).start()
    gate_load.start()
    gain_load.start()

    for b in range(NB):
        dec = decay_ref[:, b * BLOCK:(b + 1) * BLOCK]
        col = lax.dot_general(lower, dec, nt, precision=HI, preferred_element_type=F32)
        cum_col[b] = col
        dec_col[b] = jnp.exp(-col)

    r2 = lax.broadcasted_iota(jnp.int32, (HALF, HALF), 0)
    c2 = lax.broadcasted_iota(jnp.int32, (HALF, HALF), 1)
    keep = r2 >= c2

    def inside(b, _):
        rows = cum_row[b]
        cols = cum_col[b]
        for h in range(LH):
            lanes = slice(h * HD, (h + 1) * HD)
            qb = q_v[ds(b, BLOCK), lanes]
            kb = k_v[ds(b, BLOCK), lanes]
            vb = v_v[ds(b, BLOCK), lanes]
            scores = lax.dot_general(qb, kb, nt, preferred_element_type=F32)
            cr = rows[h:h + 1, :]
            cc = jnp.broadcast_to(cols[:, h:h + 1], (BLOCK, HALF))
            top = jnp.where(keep, scores[:HALF, :HALF] * jnp.exp(cr[:, :HALF] - cc[:HALF]), 0.0)
            bl = scores[HALF:, :HALF] * jnp.exp(cr[:, :HALF] - cc[HALF:])
            br = jnp.where(keep, scores[HALF:, HALF:] * jnp.exp(cr[:, HALF:] - cc[HALF:]), 0.0)
            a0 = jnp.dot(top.astype(BF16), vb[:HALF], preferred_element_type=F32)
            bottom = jnp.concatenate([bl.astype(BF16), br.astype(BF16)], axis=1)
            a1 = jnp.dot(bottom, vb, preferred_element_type=F32)
            intra[b, :HALF, lanes] = a0
            intra[b, HALF:, lanes] = a1
        return 0

    q_load.wait()
    lax.fori_loop(0, 2, inside, 0)

    def prefix(s, state):
        prefix_out[s] = state.astype(BF16)
        dec = jnp.sum(scan_in[s, SL:MSG].astype(F32), axis=0, keepdims=True)
        return dec * state + scan_in[s, 0:SL].astype(F32)

    all_of(scan_in.at[0:N_CTX - 1], scan_sem.at[1])
    lax.fori_loop(0, N_CTX, prefix, jnp.zeros((SL, HD), F32))
    for dy in far_first:
        for dx in far_first:
            if dy == 0 and dx == 0:
                prefix_in[ctx] = prefix_out[ctx]
            else:
                prefix_copy((ctx_y + dy) % 4 * 4 + (ctx_x + dx) % 4, ctx).start()

    lax.fori_loop(2, NB, inside, 0)

    def gating(b, _):
        for h in range(LH):
            lanes = slice(h * HD, (h + 1) * HD)
            gl = gate_v[ds(b, BLOCK), lanes].astype(F32)
            gated[b, :, lanes] = jax.nn.sigmoid(gl) * gain_ref[:, lanes]
        return 0

    gate_load.wait()
    gain_load.wait()
    lax.fori_loop(0, NB, gating, 0)

    all_of(prefix_in.at[0:N_CTX - 1], scan_sem.at[3])

    ones = jnp.ones((8, HD), F32)

    def ssq_copy(there, slot):
        return pltpu.make_async_remote_copy(
            src_ref=ssq_out.at[there], dst_ref=ssq_in.at[slot],
            send_sem=scan_sem.at[4], recv_sem=scan_sem.at[5],
            device_id={"head": there}, device_id_type=pl.DeviceIdType.MESH)

    def finish(rb):
        dc = dec_col[rb]
        bd = before_dec[rb]
        square = jnp.zeros((BLOCK, HD), F32)
        for h in range(LH):
            lanes = slice(h * HD, (h + 1) * HD)
            carried = jnp.concatenate([prefix_in[2 * h], prefix_in[2 * h + 1]], axis=0)
            start = (bd[h:h + 1] * carried.astype(F32) + local[rb, h // 2, h % 2]).astype(BF16)
            qb = q_v[ds(rb, BLOCK), lanes]
            inter = jnp.dot(qb, start, preferred_element_type=F32)
            attn = intra[rb, :, lanes] + dc[:, h:h + 1] * inter
            square = square + attn * attn
            hidden = (attn * gated[rb, :, lanes]).astype(BF16)
            hid[rb, ds(1 - core, HALF), lanes] = hidden[:HALF]
            hid[rb, ds(core, HALF), lanes] = hidden[HALF:]
        sums = lax.dot_general(ones, square, nt, precision=HI, preferred_element_type=F32)
        for s in range(2):
            there = rb * 2 + s
            ssq_out[there] = sums[:, s * HALF:(s + 1) * HALF]

            @pl.when(there != head)
            def _():
                ssq_copy(there, head).start()

            @pl.when(there == head)
            def _():
                ssq_in[head] = ssq_out[head]

    def core_copy(phase, lane, j):
        slot = phase * NC + lane * NH + j
        return pltpu.make_async_remote_copy(
            src_ref=core_out.at[slot], dst_ref=core_in.at[slot],
            send_sem=core_ssem, recv_sem=core_rsem.at[lane, (phase * NH + j) % 4],
            device_id={"head": partner}, device_id_type=pl.DeviceIdType.MESH)

    def far_copy(n, there):
        return pltpu.make_async_remote_copy(
            src_ref=z_out.at[0, n], dst_ref=far_in.at[n],
            send_sem=z_ssem, recv_sem=far_rsem.at[n // 2],
            device_id={"head": there}, device_id_type=pl.DeviceIdType.MESH)

    def near_copy(side, n, there, sem):
        return pltpu.make_async_remote_copy(
            src_ref=z_out.at[1 + side, n], dst_ref=near_in.at[side, n],
            send_sem=z_ssem, recv_sem=sem,
            device_id={"head": there}, device_id_type=pl.DeviceIdType.MESH)

    def product(phase, lane, j, rb, n):
        r = jnp.dot(hid[rb], w_v[n], preferred_element_type=F32)
        core_out[phase * NC + lane * NH + j] = r[:HALF].astype(BF16)
        core_copy(phase, lane, j).start()
        return r[HALF:]

    def summed(phase, lane, j):
        core_copy(phase, lane, j).wait_recv()
        return own[lane] + core_in[phase * NC + lane * NH + j].astype(F32)

    def fin0(lane, j):
        n = lane * NH + j
        z_out[0, n] = summed(0, lane, j).astype(BF16)
        far_copy(n, right if lane == 0 else left).start()

    def fin1(lane, j):
        n = (1 - lane) * NH + j
        z_out[1 + lane, n] = summed(1, lane, j).astype(BF16)
        near_copy(lane, n, right if lane == 0 else left, early_rsem.at[lane]).start()

    def fin2(lane, j):
        n = lane * NH + j
        s = summed(2, lane, j)

        @pl.when(j % 2 == 0)
        def _():
            all_of(far_in.at[pl.ds(n, 2)], far_rsem.at[n // 2])

        z_out[1 + lane, n] = (s + far_in[n].astype(F32)).astype(BF16)
        near_copy(lane, n, right if lane == 0 else left, late_rsem.at[lane, j]).start()

    def keep_total(n, value):
        intra[n // 4, ds(n // 2 % 2, HALF), ds(n % 2, CN)] = value

    def kept_total(n):
        return intra[n // 4, ds(n // 2 % 2, HALF), ds(n % 2, CN)]

    def fin3(lane, j):
        n = lane * NH + j
        keep_total(n, summed(3, lane, j))

    def step(phase, lane, j):
        n = (1 - lane) * NH + j if phase == 1 else lane * NH + j
        if phase == 0:
            rb = zo
        elif phase == 3:
            rb = z
        else:
            rb = zr if lane == 0 else zl
        return product(phase, lane, j, rb, n)

    fins = (fin0, fin1, fin2, fin3)
    pending = None
    for phase in range(4):
        if phase == 0:
            finish(zo)
            all_of(w_v, once_sem.at[4])
        elif phase == 1:
            finish(zr)
            finish(zl)
        elif phase == 3:
            finish(z)
        for lane in range(2):
            r = step(phase, lane, 0)
            if pending is not None:
                pending(lane, NH - 1)
            own[lane] = r

        def body(j, _, phase=phase):
            for lane in range(2):
                r = step(phase, lane, j)
                fins[phase](lane, j - 1)
                own[lane] = r
            return 0

        lax.fori_loop(1, NH, body, 0)
        pending = fins[phase]
    for lane in range(2):
        pending(lane, NH - 1)

    all_of(ssq_in.at[0:N_HEAD - 1], scan_sem.at[5])
    squares = jnp.sum(ssq_in[...], axis=0)
    scale_row = lax.rsqrt(squares[0:1, :] * (1.0 / (HEADS * HD)) + EPS)
    scale = jnp.sum(
        jnp.where(r2 == c2, jnp.broadcast_to(scale_row, (HALF, HALF)), 0.0), axis=1, keepdims=True)

    all_of(near_in.at[0, NH:NC], early_rsem.at[0])
    all_of(near_in.at[1, 0:NH], early_rsem.at[1])

    def result(j, _):
        for lane in range(2):
            n = lane * NH + j
            near_copy(lane, n, right, late_rsem.at[lane, j]).wait_recv()
            s = kept_total(n) + near_in[0, n].astype(F32) + near_in[1, n].astype(F32)
            out_ref[:, ds(n, CN)] = (s * scale).astype(BF16)
        return 0

    lax.fori_loop(0, NH, result, 0)

    all_of(scan_out.at[0:N_CTX - 1], scan_sem.at[0])
    all_of(prefix_out.at[0:N_CTX - 1], scan_sem.at[2])
    all_of(ssq_out.at[0:N_HEAD - 1], scan_sem.at[4])
    all_of(core_out, core_ssem)
    all_of(z_out, z_ssem)


def shards(queries, keys, values, gate_logits, log_decay, norm_gain_vector, out_weight):
    any_spec = pl.BlockSpec(memory_space=pl.ANY)
    vmem = pl.BlockSpec(memory_space=pltpu.VMEM)
    dma = pltpu.SemaphoreType.DMA
    return pl.pallas_call(
        kernel,
        out_shape=pltpu.VMEM((ROWS // N_HEAD, D), BF16),
        in_specs=[any_spec] * 7,
        out_specs=vmem,
        scratch_shapes=[
            pltpu.VMEM((LH, ROWS), F32),
            pltpu.VMEM((1, WIDTH), F32),
            pltpu.VMEM((ROWS, WIDTH), BF16),
            pltpu.VMEM((ROWS, WIDTH), BF16),
            pltpu.VMEM((ROWS, WIDTH), BF16),
            pltpu.VMEM((ROWS, WIDTH), BF16),
            pltpu.VMEM((NC, WIDTH, CN), BF16),
            pltpu.VMEM((NB, BLOCK, WIDTH), BF16),
            pltpu.VMEM((NB, BLOCK, WIDTH), F32),
            pltpu.VMEM((NB, BLOCK, WIDTH), F32),
            pltpu.VMEM((NB, 4, 2, HD, HD), F32),
            pltpu.VMEM((NB, LH, BLOCK), F32),
            pltpu.VMEM((NB, BLOCK, LH), F32),
            pltpu.VMEM((NB, BLOCK, LH), F32),
            pltpu.VMEM((NB, LH, HD), F32),
            pltpu.VMEM((NB, 4, 2, BLOCK), F32),
            pltpu.VMEM((NB, 4, 2, HD), F32),
            pltpu.VMEM((4, 2, 16, HD), BF16),
            pltpu.VMEM((N_CTX, MSG, HD), BF16),
            pltpu.VMEM((N_CTX, MSG, HD), BF16),
            pltpu.VMEM((N_CTX, SL, HD), BF16),
            pltpu.VMEM((N_CTX, SL, HD), BF16),
            pltpu.VMEM((N_HEAD, 8, HALF), F32),
            pltpu.VMEM((N_HEAD, 8, HALF), F32),
            pltpu.VMEM((4 * NC, HALF, CN), BF16),
            pltpu.VMEM((4 * NC, HALF, CN), BF16),
            pltpu.VMEM((2, HALF, CN), F32),
            pltpu.VMEM((3, NC, HALF, CN), BF16),
            pltpu.VMEM((NC, HALF, CN), BF16),
            pltpu.VMEM((2, NC, HALF, CN), BF16),
            dma((2, NB)), dma((5,)), dma((6,)),
            dma, dma((2, 4)),
            dma, dma((NC // 2,)), dma((2,)), dma((2, NH)),
        ],
        compiler_params=pltpu.CompilerParams(
            collective_id=0, has_side_effects=True, vmem_limit_bytes=60 * 1024 * 1024),
        cost_estimate=pl.CostEstimate(
            flops=15_000_000_000, bytes_accessed=23_000_000, transcendentals=4_000_000),
        name="attention",
    )(queries, keys, values, gate_logits, log_decay, norm_gain_vector.reshape(1, WIDTH), out_weight)


def solution(mesh):
    in_specs = (
        P("ctx", "head"),
        P("ctx", "head"),
        P("ctx", "head"),
        P("ctx", "head"),
        P("head", "ctx"),
        P("head"),
        P("head", None),
    )
    out_specs = P(("ctx", "head"), None)
    return jax.shard_map(shards, mesh=mesh, in_specs=in_specs, out_specs=out_specs, check_vma=False)
```

time: 85.3 us -> 80.4 us (0.943)
  Pallas kernels: 82.4 us -> 79.1 us
  local copies, waits for them, and re-layouts: 2.69 us -> 1.15 us
    pallas_call x1, Pallas kernels: 82.4 us -> 79.1 us  [shards(): pl.pallas_call(kernel, out_shape=pltpu.VMEM((ROWS // N_HEAD, D), BF16), i...]
    unnamed x1, local copies, waits for them, and re-layouts: 2.69 us -> 1.15 us
where the time goes in v2:
time: 80.4 us; the launch traced here: 80.3 us
  Pallas kernels  79.1 us (98%)
  local copies, waits for them, and re-layouts  1.15 us (1%)
    pallas_call x1, Pallas kernels, shards(): pl.pallas_call(kernel, out_shape=pltpu.VMEM((ROWS // N_HEAD, D), BF16), i...  79.1 us

profile of v2, /device:TPU:1, one launch (start us, length us, event | category | flops | bytes accessed | tf_op | source)
XLA Modules:
  0.0 80.3 jit_solution(15711405447744494368)
XLA Ops:
  0.0 79.1 %attention.1 = bf16[128,6144]{1,0:T(8,128)(2,1)S(1)} custom-call(bf16[1024,1024]{1,0:T(8,128)(2,1)} %q_hbm.1, bf16[1024,1024]{1,0:T(8,128)(2,1)} %k_hbm.1, bf16[1024,1024]{1,0:T(8,128)(2,1)} %v_hbm.1, bf16[1024,1024]{1,0:T(8,128)(2,1)} %gate_hbm.1, f32[8,1024]{1,0:T(8,128)} %decay_hbm.1, f32[1,1024]{1,0:T(1,128)} %bitcast.1, bf16[1024,6144]{1,0:T(8,128)(2,1)} %w_hbm.1), custom_call_target="tpu_custom_call" | custom-call | flops 15000000512 | bytes 23000000 | tf_op jit(solution)/shard_map/attention/pallas_call | solution.py:416
  79.1 1.1 %copy.9 = bf16[128,6144]{1,0:T(8,128)(2,1)} copy(bf16[128,6144]{1,0:T(8,128)(2,1)S(1)} %attention.1) | data formatting | bytes 3145728

commit v3 on v2

--- a/solution.py
+++ b/solution.py
@@ -40,10 +40,10 @@
     q_hbm, k_hbm, v_hbm, gate_hbm, decay_hbm, gain_hbm, w_hbm, out_ref,
     decay_ref, gain_ref,
     q_v, k_v, v_v, gate_v, w_v, hid, intra, gated, local,
-    cum_row, cum_col, dec_col, before_dec, factor, keep_dec, parts,
+    cum_row, cum_col, before_dec, factor, keep_dec, parts,
     scan_out, scan_in, prefix_out, prefix_in, ssq_out, ssq_in,
     core_out, core_in, own, z_out, far_in, near_in,
-    load_sem, once_sem, scan_sem, core_ssem, core_rsem, z_ssem, far_rsem, early_rsem, late_rsem,
+    load_sem, once_sem, scan_sem, scan_rsem, carried_sem, core_ssem, core_rsem, z_ssem, far_rsem, early_rsem, late_rsem,
 ):
     ctx = lax.axis_index("ctx")
     head = lax.axis_index("head")
@@ -78,23 +78,23 @@
     ctx_x = ctx % 4
     far_first = (2, 1, 3, 0)
     pairs = [(ctx_y + off) % 4 for off in far_first]
+    barrier = pltpu.get_barrier_semaphore()
+    for dy in far_first:
+        for dx in far_first:
+            if dy or dx:
+                pl.semaphore_signal(
+                    barrier, inc=1, device_id={"ctx": (ctx_y + dy) % 4 * 4 + (ctx_x + dx) % 4},
+                    device_id_type=pl.DeviceIdType.MESH)
+
     for b in range(NB):
         block_load(0, k_hbm, k_v, b).start()
         block_load(1, v_hbm, v_v, b).start()
-
-    barrier = pltpu.get_barrier_semaphore()
-
-    def greet_ctx(d, _):
-        pl.semaphore_signal(barrier, inc=1, device_id={"ctx": (ctx + d) % N_CTX},
-                            device_id_type=pl.DeviceIdType.MESH)
-        return 0
 
     def greet_head(d, _):
         pl.semaphore_signal(barrier, inc=1, device_id={"head": (head + d) % N_HEAD},
                             device_id_type=pl.DeviceIdType.MESH)
         return 0
 
-    lax.fori_loop(1, N_CTX, greet_ctx, 0)
     lax.fori_loop(1, N_HEAD, greet_head, 0)
 
     ri = lax.broadcasted_iota(jnp.int32, (BLOCK, BLOCK), 0)
@@ -103,20 +103,26 @@
     eye = (ri == ci).astype(BF16)
     nt = (((1,), (1,)), ((), ()))
     before = jnp.zeros((LH, 1), F32)
+    tile = lax.broadcasted_iota(jnp.int32, (16, HD), 0)
     decay_load.wait()
-    tile = lax.broadcasted_iota(jnp.int32, (16, HD), 0)
+    blocks = jnp.concatenate([decay_ref[:, b * BLOCK:(b + 1) * BLOCK] for b in range(NB)], axis=0)
+    high = blocks.astype(BF16).astype(F32)
+    middle = (blocks - high).astype(BF16).astype(F32)
+    thirds = jnp.concatenate([high, middle, blocks - high - middle], axis=0).astype(BF16)
+    sums = lax.dot_general(thirds, lower.astype(BF16), nt, preferred_element_type=F32)
+    all_rows = sums[:NB * LH] + (sums[NB * LH:2 * NB * LH] + sums[2 * NB * LH:])
     for b in range(NB):
-        dec = decay_ref[:, b * BLOCK:(b + 1) * BLOCK]
-        row = lax.dot_general(dec, lower, nt, precision=HI, preferred_element_type=F32)
+        row = all_rows[b * LH:(b + 1) * LH]
         cum_row[b] = row
         last = row[:, BLOCK - 1:BLOCK]
         fac = jnp.exp(row - last)
         kept = jnp.broadcast_to(jnp.exp(-last), (LH, HD))
-        before_dec[b] = jnp.broadcast_to(jnp.exp(-before), (LH, HD))
+        entry = jnp.broadcast_to(jnp.exp(-before), (LH, HD))
         before = before + last
         for p in range(4):
             factor[b, p] = fac[2 * p:2 * p + 2]
             keep_dec[b, p] = kept[2 * p:2 * p + 2]
+            before_dec[b, p] = entry[2 * p:2 * p + 2]
     shard_dec = jnp.broadcast_to(jnp.exp(-before), (LH, HD))
     for h in range(LH):
         a = jnp.broadcast_to(shard_dec[h:h + 1], (16, HD))
@@ -129,13 +135,13 @@
     def scan_copy(there, slot):
         return pltpu.make_async_remote_copy(
             src_ref=scan_out.at[there], dst_ref=scan_in.at[slot],
-            send_sem=scan_sem.at[0], recv_sem=scan_sem.at[1],
+            send_sem=scan_sem.at[0], recv_sem=scan_rsem.at[ctx_y],
             device_id={"ctx": there}, device_id_type=pl.DeviceIdType.MESH)
 
     def prefix_copy(there, slot):
         return pltpu.make_async_remote_copy(
             src_ref=prefix_out.at[there], dst_ref=prefix_in.at[slot],
-            send_sem=scan_sem.at[2], recv_sem=scan_sem.at[3],
+            send_sem=scan_sem.at[2], recv_sem=carried_sem.at[ctx_y],
             device_id={"ctx": there}, device_id_type=pl.DeviceIdType.MESH)
 
     def added(b, p):
@@ -179,23 +185,15 @@
             else:
                 scan_copy(there, ctx).start()
 
-    for j in range(NH):
-        w_load(j).start()
-        w_load(NH + j).start()
-    gate_load.start()
-    gain_load.start()
-
+    all_cols = lax.dot_general(lower, blocks, nt, precision=HI, preferred_element_type=F32)
     for b in range(NB):
-        dec = decay_ref[:, b * BLOCK:(b + 1) * BLOCK]
-        col = lax.dot_general(lower, dec, nt, precision=HI, preferred_element_type=F32)
-        cum_col[b] = col
-        dec_col[b] = jnp.exp(-col)
+        cum_col[b] = all_cols[:, b * LH:(b + 1) * LH]
 
     r2 = lax.broadcasted_iota(jnp.int32, (HALF, HALF), 0)
     c2 = lax.broadcasted_iota(jnp.int32, (HALF, HALF), 1)
     keep = r2 >= c2
 
-    def inside(b, _):
+    def inside(b):
         rows = cum_row[b]
         cols = cum_col[b]
         for h in range(LH):
@@ -214,63 +212,83 @@
             a1 = jnp.dot(bottom, vb, preferred_element_type=F32)
             intra[b, :HALF, lanes] = a0
             intra[b, HALF:, lanes] = a1
-        return 0
+            q_v[ds(b, BLOCK), lanes] = (qb.astype(F32) * jnp.exp(-cc)).astype(BF16)
+
+    def prefixes(y, state):
+        for own_row in (False, True):
+            @pl.when((ctx_y == y) == own_row)
+            def _():
+                all_of(scan_in.at[0:3 if own_row else 4], scan_rsem.at[y])
+
+        for s in range(4 * y, 4 * y + 4):
+            if s < N_CTX - 1:
+                dec = jnp.sum(scan_in[s, SL:MSG].astype(F32), axis=0, keepdims=True)
+                state = dec * state + scan_in[s, 0:SL].astype(F32)
+                prefix_out[s + 1] = state.astype(BF16)
+        for s in range(4 * y + 1, min(4 * y + 5, N_CTX)):
+            @pl.when(s != ctx)
+            def _():
+                prefix_copy(s, ctx).start()
+        return state
 
     q_load.wait()
-    lax.fori_loop(0, 2, inside, 0)
-
-    def prefix(s, state):
-        prefix_out[s] = state.astype(BF16)
-        dec = jnp.sum(scan_in[s, SL:MSG].astype(F32), axis=0, keepdims=True)
-        return dec * state + scan_in[s, 0:SL].astype(F32)
-
-    all_of(scan_in.at[0:N_CTX - 1], scan_sem.at[1])
-    lax.fori_loop(0, N_CTX, prefix, jnp.zeros((SL, HD), F32))
-    for dy in far_first:
-        for dx in far_first:
-            if dy == 0 and dx == 0:
-                prefix_in[ctx] = prefix_out[ctx]
-            else:
-                prefix_copy((ctx_y + dy) % 4 * 4 + (ctx_x + dx) % 4, ctx).start()
-
-    lax.fori_loop(2, NB, inside, 0)
-
-    def gating(b, _):
+    gate_load.start()
+    gain_load.start()
+    for j in range(NH):
+        w_load(j).start()
+        w_load(NH + j).start()
+    state = jnp.zeros((SL, HD), F32)
+    for y in range(4):
+        state = prefixes(y, state)
+
+    @pl.when(ctx == 0)
+    def _():
+        prefix_in[...] = jnp.zeros_like(prefix_in)
+
+    @pl.when(ctx != 0)
+    def _():
+        prefix_in[ctx] = prefix_out[ctx]
+
+    def gating(b):
         for h in range(LH):
             lanes = slice(h * HD, (h + 1) * HD)
             gl = gate_v[ds(b, BLOCK), lanes].astype(F32)
             gated[b, :, lanes] = jax.nn.sigmoid(gl) * gain_ref[:, lanes]
-        return 0
 
     gate_load.wait()
     gain_load.wait()
-    lax.fori_loop(0, NB, gating, 0)
-
-    all_of(prefix_in.at[0:N_CTX - 1], scan_sem.at[3])
+    inside(zo)
+    gating(zo)
 
     ones = jnp.ones((8, HD), F32)
 
     def ssq_copy(there, slot):
         return pltpu.make_async_remote_copy(
             src_ref=ssq_out.at[there], dst_ref=ssq_in.at[slot],
-            send_sem=scan_sem.at[4], recv_sem=scan_sem.at[5],
+            send_sem=scan_sem.at[3], recv_sem=scan_sem.at[4],
             device_id={"head": there}, device_id_type=pl.DeviceIdType.MESH)
 
-    def finish(rb):
-        dc = dec_col[rb]
-        bd = before_dec[rb]
+    def finish(rb, first=False):
         square = jnp.zeros((BLOCK, HD), F32)
-        for h in range(LH):
-            lanes = slice(h * HD, (h + 1) * HD)
-            carried = jnp.concatenate([prefix_in[2 * h], prefix_in[2 * h + 1]], axis=0)
-            start = (bd[h:h + 1] * carried.astype(F32) + local[rb, h // 2, h % 2]).astype(BF16)
-            qb = q_v[ds(rb, BLOCK), lanes]
-            inter = jnp.dot(qb, start, preferred_element_type=F32)
-            attn = intra[rb, :, lanes] + dc[:, h:h + 1] * inter
-            square = square + attn * attn
-            hidden = (attn * gated[rb, :, lanes]).astype(BF16)
-            hid[rb, ds(1 - core, HALF), lanes] = hidden[:HALF]
-            hid[rb, ds(core, HALF), lanes] = hidden[HALF:]
+        for i, p in enumerate((ctx_y + off) % 4 for off in (0, 1, 3, 2)):
+            if first:
+                @pl.when(ctx != 0)
+                def _(i=i, p=p):
+                    all_of(prefix_in.at[0:4 - (1 if i == 0 else 0)], carried_sem.at[p])
+
+            for s in range(2):
+                lanes = ds(2 * p + s, HD)
+                carried = jnp.concatenate([prefix_in[4 * p + 2 * s], prefix_in[4 * p + 2 * s + 1]], axis=0)
+                start = before_dec[rb, p, s:s + 1, :] * carried.astype(F32) + local[rb, p, s]
+                inter = jnp.dot(q_v[ds(rb, BLOCK), lanes], start.astype(BF16), preferred_element_type=F32)
+                attn = intra[rb, :, lanes] + inter
+                square = square + attn * attn
+                hidden = (attn * gated[rb, :, lanes]).astype(BF16)
+                hid[rb, ds(1 - core, HALF), lanes] = hidden[:HALF]
+                hid[rb, ds(core, HALF), lanes] = hidden[HALF:]
+        return square
+
+    def send_squares(rb, square):
         sums = lax.dot_general(ones, square, nt, precision=HI, preferred_element_type=F32)
         for s in range(2):
             there = rb * 2 + s
@@ -358,13 +376,18 @@
     pending = None
     for phase in range(4):
         if phase == 0:
-            finish(zo)
+            square = finish(zo, first=True)
             all_of(w_v, once_sem.at[4])
         elif phase == 1:
-            finish(zr)
-            finish(zl)
+            send_squares(zo, square)
+            for rb in (zr, zl):
+                inside(rb)
+                gating(rb)
+                send_squares(rb, finish(rb))
         elif phase == 3:
-            finish(z)
+            inside(z)
+            gating(z)
+            send_squares(z, finish(z))
         for lane in range(2):
             r = step(phase, lane, 0)
             if pending is not None:
@@ -383,7 +406,7 @@
     for lane in range(2):
         pending(lane, NH - 1)
 
-    all_of(ssq_in.at[0:N_HEAD - 1], scan_sem.at[5])
+    all_of(ssq_in.at[0:N_HEAD - 1], scan_sem.at[4])
     squares = jnp.sum(ssq_in[...], axis=0)
     scale_row = lax.rsqrt(squares[0:1, :] * (1.0 / (HEADS * HD)) + EPS)
     scale = jnp.sum(
@@ -403,8 +426,13 @@
     lax.fori_loop(0, NH, result, 0)
 
     all_of(scan_out.at[0:N_CTX - 1], scan_sem.at[0])
-    all_of(prefix_out.at[0:N_CTX - 1], scan_sem.at[2])
-    all_of(ssq_out.at[0:N_HEAD - 1], scan_sem.at[4])
+    all_of(prefix_out.at[0:N_CTX - 2], scan_sem.at[2])
+
+    @pl.when(ctx == 0)
+    def _():
+        all_of(prefix_out.at[0:1], scan_sem.at[2])
+
+    all_of(ssq_out.at[0:N_HEAD - 1], scan_sem.at[3])
     all_of(core_out, core_ssem)
     all_of(z_out, z_ssem)
 
@@ -432,8 +460,7 @@
             pltpu.VMEM((NB, 4, 2, HD, HD), F32),
             pltpu.VMEM((NB, LH, BLOCK), F32),
             pltpu.VMEM((NB, BLOCK, LH), F32),
-            pltpu.VMEM((NB, BLOCK, LH), F32),
-            pltpu.VMEM((NB, LH, HD), F32),
+            pltpu.VMEM((NB, 4, 2, HD), F32),
             pltpu.VMEM((NB, 4, 2, BLOCK), F32),
             pltpu.VMEM((NB, 4, 2, HD), F32),
             pltpu.VMEM((4, 2, 16, HD), BF16),
@@ -449,7 +476,7 @@
             pltpu.VMEM((3, NC, HALF, CN), BF16),
             pltpu.VMEM((NC, HALF, CN), BF16),
             pltpu.VMEM((2, NC, HALF, CN), BF16),
-            dma((2, NB)), dma((5,)), dma((6,)),
+            dma((2, NB)), dma((5,)), dma((5,)), dma((4,)), dma((4,)),
             dma, dma((2, 4)),
             dma, dma((NC // 2,)), dma((2,)), dma((2, NH)),
         ],

time: 80.4 us -> 75.7 us (0.942)
  Pallas kernels: 79.1 us -> 73.6 us
    pallas_call x1, Pallas kernels: 79.1 us -> 73.6 us  [shards(): pl.pallas_call(kernel, out_shape=pltpu.VMEM((ROWS // N_HEAD, D), BF16), i...]
where the time goes in v3:
time: 75.7 us; the launch traced here: 74.8 us
  Pallas kernels  73.6 us (97%)
  local copies, waits for them, and re-layouts  1.15 us (2%)
    pallas_call x1, Pallas kernels, shards(): pl.pallas_call(kernel, out_shape=pltpu.VMEM((ROWS // N_HEAD, D), BF16), i...  73.6 us

profile of v3, /device:TPU:1, one launch (start us, length us, event | category | flops | bytes accessed | tf_op | source)
XLA Modules:
  0.0 74.8 jit_solution(1835280972600994228)
XLA Ops:
  0.0 73.6 %attention.1 = bf16[128,6144]{1,0:T(8,128)(2,1)S(1)} custom-call(bf16[1024,1024]{1,0:T(8,128)(2,1)} %q_hbm.1, bf16[1024,1024]{1,0:T(8,128)(2,1)} %k_hbm.1, bf16[1024,1024]{1,0:T(8,128)(2,1)} %v_hbm.1, bf16[1024,1024]{1,0:T(8,128)(2,1)} %gate_hbm.1, f32[8,1024]{1,0:T(8,128)} %decay_hbm.1, f32[1,1024]{1,0:T(1,128)} %bitcast.1, bf16[1024,6144]{1,0:T(8,128)(2,1)} %w_hbm.1), custom_call_target="tpu_custom_call" | custom-call | flops 15000000512 | bytes 23000000 | tf_op jit(solution)/shard_map/attention/pallas_call | solution.py:444
  73.6 1.1 %copy.9 = bf16[128,6144]{1,0:T(8,128)(2,1)} copy(bf16[128,6144]{1,0:T(8,128)(2,1)S(1)} %attention.1) | data formatting | bytes 3145728

commit v4 on v3

--- a/solution.py
+++ b/solution.py
@@ -177,6 +177,9 @@
                 scan_out[4 * p + 2 * s + t, 0:SL] = state[t * SL:(t + 1) * SL].astype(BF16)
                 scan_out[4 * p + 2 * s + t, SL:MSG] = parts[p, s]
         if i == 0:
+            for j in range(NH):
+                w_load(j).start()
+                w_load(NH + j).start()
             pl.semaphore_wait(barrier, N_CTX - 1 + N_HEAD - 1)
         for off in far_first:
             there = 4 * p + (ctx_x + off) % 4
@@ -225,7 +228,7 @@
                 dec = jnp.sum(scan_in[s, SL:MSG].astype(F32), axis=0, keepdims=True)
                 state = dec * state + scan_in[s, 0:SL].astype(F32)
                 prefix_out[s + 1] = state.astype(BF16)
-        for s in range(4 * y + 1, min(4 * y + 5, N_CTX)):
+        for s in ([4 * y + 4] if y < 3 else []) + [4 * y + 1, 4 * y + 2, 4 * y + 3]:
             @pl.when(s != ctx)
             def _():
                 prefix_copy(s, ctx).start()
@@ -234,9 +237,6 @@
     q_load.wait()
     gate_load.start()
     gain_load.start()
-    for j in range(NH):
-        w_load(j).start()
-        w_load(NH + j).start()
     state = jnp.zeros((SL, HD), F32)
     for y in range(4):
         state = prefixes(y, state)

time: 75.7 us -> 75.6 us (level)
  no operation moved by 1% of the time
where the time goes in v4:
time: 75.6 us; the launch traced here: 74.8 us
  Pallas kernels  73.6 us (97%)
  local copies, waits for them, and re-layouts  1.15 us (2%)
    pallas_call x1, Pallas kernels, shards(): pl.pallas_call(kernel, out_shape=pltpu.VMEM((ROWS // N_HEAD, D), BF16), i...  73.6 us

profile of v4, /device:TPU:1, one launch (start us, length us, event | category | flops | bytes accessed | tf_op | source)
XLA Modules:
  0.0 74.8 jit_solution(10126986067127686249)
XLA Ops:
  0.0 73.6 %attention.1 = bf16[128,6144]{1,0:T(8,128)(2,1)S(1)} custom-call(bf16[1024,1024]{1,0:T(8,128)(2,1)} %q_hbm.1, bf16[1024,1024]{1,0:T(8,128)(2,1)} %k_hbm.1, bf16[1024,1024]{1,0:T(8,128)(2,1)} %v_hbm.1, bf16[1024,1024]{1,0:T(8,128)(2,1)} %gate_hbm.1, f32[8,1024]{1,0:T(8,128)} %decay_hbm.1, f32[1,1024]{1,0:T(1,128)} %bitcast.1, bf16[1024,6144]{1,0:T(8,128)(2,1)} %w_hbm.1), custom_call_target="tpu_custom_call" | custom-call | flops 15000000512 | bytes 23000000 | tf_op jit(solution)/shard_map/attention/pallas_call | solution.py:444
  73.6 1.1 %copy.9 = bf16[128,6144]{1,0:T(8,128)(2,1)} copy(bf16[128,6144]{1,0:T(8,128)(2,1)S(1)} %attention.1) | data formatting | bytes 3145728
